TPU v7x, 256 devices: a whole 4x4x8 slice. The times are simulated.
256 devices in a mesh: dp: 32 (over x, y, core), tp: 8 (over z).
Axes of the slice: x: 4, y: 4, z: 8, core: 2. Of those that a mesh axis runs over, the one named last changes fastest.
Arguments:
- queries: bfloat16 [1024, 24576], P('dp', 'tp')
- latent_cache: bfloat16 [1024, 256, 576], P('dp')
- fresh_latent_entry: bfloat16 [1024, 576], P('dp'), may hold values from -6 to 6
- lengths: int32 [1024], P('dp'), may hold values from 2 to 256, as said below
- key_up_matrix: bfloat16 [128, 128, 512], P('tp'), may hold values from -0.5 to 0.5
- value_up_matrix: bfloat16 [128, 512, 128], P('tp'), may hold values from -0.25 to 0.25
- out_proj: bfloat16 [16384, 7168], P('dp', 'tp'), may hold values from -0.09375 to 0.09375
- residual: bfloat16 [1024, 7168], P('dp', 'tp'), may hold values from -6 to 6
- norm_gain: bfloat16 [7168], P('tp'), may hold values from 0.099609375 to 1.8984375
- gate_weight: bfloat16 [7168, 18432], P('tp', 'dp'), may hold values from -0.0625 to 0.0625
- up_weight: bfloat16 [7168, 18432], P('tp', 'dp'), may hold values from -0.0625 to 0.0625
- down_weight: bfloat16 [18432, 7168], P('dp', 'tp'), may hold values from -0.09375 to 0.09375
Outputs:
- layer_out: bfloat16 [1024, 7168], P('dp', 'tp')
Inputs may be any that keep to these rules, and one draw needn't show every extreme that they name: The used slots of a request are its first lengths[r]; some request uses all 256.
All inputs are finite; a program needn't handle non-finite values.
Results may differ from a plain program's by a relative error of at most 0.015.
Values may be sent and summed in bfloat16 or wider, within the bound.
A program may use at most 128 MiB of HBM per device.

v0:
```python
import jax
import jax.numpy as jnp
from jax import lax
from jax.sharding import PartitionSpec as P

D = 7168


def normalize(stream, norm_gain):
    stream_f = stream.astype(jnp.float32)
    square_total = lax.psum(jnp.sum(stream_f * stream_f, axis=1), "tp")
    mean_square = square_total / D
    scaled = (
        stream_f * lax.rsqrt(mean_square + 1e-06)[:, None] * norm_gain.astype(jnp.float32)[None, :]
    )
    return scaled.astype(jnp.bfloat16)


def body(
    queries,
    latent_cache,
    fresh_latent_entry,
    lengths,
    key_up_matrix,
    value_up_matrix,
    out_proj,
    residual,
    norm_gain,
    gate_weight,
    up_weight,
    down_weight,
):
    own_rows = queries.shape[0]
    head_count, nope_width, latent_width = key_up_matrix.shape
    rope_width = latent_cache.shape[2] - latent_width
    value_width = value_up_matrix.shape[2]
    slot_count = latent_cache.shape[1]
    score_scale = 1.0 / (nope_width + rope_width) ** 0.5
    query_heads = queries.reshape(own_rows, head_count, nope_width + rope_width)
    q_latent = jnp.einsum(
        "rhk,hkl->rhl",
        query_heads[:, :, :nope_width],
        key_up_matrix,
        preferred_element_type=jnp.float32,
    ).astype(jnp.bfloat16)
    q_full = jnp.concatenate([q_latent, query_heads[:, :, nope_width:]], axis=2)
    scores = (
        jnp.einsum("rhc,rjc->rhj", q_full, latent_cache, preferred_element_type=jnp.float32)
        * score_scale
    )
    new_score = (
        jnp.einsum("rhc,rc->rh", q_full, fresh_latent_entry, preferred_element_type=jnp.float32)
        * score_scale
    )
    slot_used = (lax.broadcasted_iota(jnp.int32, (own_rows, slot_count), 1) < lengths[:, None])[
        :, None, :
    ]
    masked = jnp.where(slot_used, scores, -1e30)
    top_score = jnp.maximum(jnp.max(masked, axis=2), new_score)
    weights = jnp.where(slot_used, jnp.exp(masked - top_score[:, :, None]), 0.0)
    new_weight = jnp.exp(new_score - top_score)
    denom = jnp.sum(weights, axis=2) + new_weight
    slot_probabilities = (weights / denom[:, :, None]).astype(jnp.bfloat16)
    fresh_token_prob = (new_weight / denom).astype(jnp.bfloat16)
    latent_result = jnp.einsum(
        "rhj,rjl->rhl",
        slot_probabilities,
        latent_cache[:, :, :latent_width],
        preferred_element_type=jnp.float32,
    )
    latent_result = latent_result + fresh_token_prob.astype(jnp.float32)[
        :, :, None
    ] * fresh_latent_entry[:, None, :latent_width].astype(jnp.float32)
    attn_latent = latent_result.astype(jnp.bfloat16)
    attn_heads = jnp.einsum(
        "rhl,hlv->rhv", attn_latent, value_up_matrix, preferred_element_type=jnp.float32
    ).astype(jnp.bfloat16)
    attn_heads = attn_heads.reshape(own_rows, head_count * value_width)
    joined = lax.all_gather(attn_heads, "tp", axis=1, tiled=True)
    blocks = lax.all_to_all(joined, "dp", split_axis=1, concat_axis=0, tiled=True)
    projected = lax.psum(jnp.dot(blocks, out_proj, preferred_element_type=jnp.float32), "dp")
    residual_all = lax.all_gather(residual, "dp", axis=0, tiled=True)
    stream_all = (residual_all.astype(jnp.float32) + projected).astype(jnp.bfloat16)
    normed_all = normalize(stream_all, norm_gain)
    stream = lax.dynamic_slice_in_dim(stream_all, lax.axis_index("dp") * own_rows, own_rows, 0)
    gate_part = jnp.dot(normed_all, gate_weight, preferred_element_type=jnp.float32)
    up_part = jnp.dot(normed_all, up_weight, preferred_element_type=jnp.float32)
    gate_act, up_act = lax.psum((gate_part, up_part), "tp")
    hidden_all = (jax.nn.silu(gate_act) * up_act).astype(jnp.bfloat16)
    mlp_out = lax.psum_scatter(
        jnp.dot(hidden_all, down_weight, preferred_element_type=jnp.float32),
        "dp",
        scatter_dimension=0,
        tiled=True,
    )
    return (stream.astype(jnp.float32) + mlp_out).astype(jnp.bfloat16)


def solution(mesh):
    return jax.shard_map(
        body,
        mesh=mesh,
        in_specs=(
            P("dp", "tp"),
            P("dp", None, None),
            P("dp", None),
            P("dp"),
            P("tp", None, None),
            P("tp", None, None),
            P("dp", "tp"),
            P("dp", "tp"),
            P("tp"),
            P("tp", "dp"),
            P("tp", "dp"),
            P("dp", "tp"),
        ),
        out_specs=P("dp", "tp"),
        check_vma=False,
    )
```

profile of v0, /device:TPU:8, one launch (start us, length us, event | category | flops | bytes accessed | tf_op | source)
XLA Modules:
  0.0 485.8 jit_solution(12669052307508138981)
XLA Ops:
  6.5 1.4 reshape.31
  8.1 0.7 iota_compare_fusion
  8.8 0.8 slice_convert_fusion
  9.6 0.4 fusion.5
  10.0 0.1 pad_maximum_fusion
  10.1 0.4 fusion.10
  10.4 5.4 %fusion.31 = (f32[32,16]{1,0:T(8,128)S(1)}, f32[32,16,256]{2,1,0:T(8,128)S(1)}) fusion(bf16[32,256,576]{1,2,0:T(8,128)(2,1)} %param.13, bf16[32,16,576]{2,0,1:T(8,128)(2,1)S(1)} %pad_maximum_fusion, pred[32,256]{1,0:T(8,128)(4,1)S(1)} %iota_compare_fusion), kind=kOutput, calls=%fused_computation.48 | convolution fusion | flops 151387648 | bytes 10561536 | tf_op jit(solution)/shard_map/rhc,rjc->rhj/dot_general | solution.py:48
  15.9 0.3 fusion.20
  16.2 0.1 slice-done.1
  16.3 0.2 slice-done.2
  16.5 2.4 fusion
  18.9 0.1 copy.18
  19.0 2.4 fusion.8
  21.4 0.7 copy.45
  22.2 0.7 all-gather.3.cloned.1.call-update
  22.9 41.0 %all-gather.5.cloned.1.call-done = bf16[32,16384]{1,0:T(8,128)(2,1)} async-done(((bf16[32,2048]{1,0:T(8,128)(2,1)}), bf16[32,16384]{1,0:T(8,128)(2,1)}) %all-gather.5.cloned.1.call-update) | async-done | bytes 1048592 | tf_op jit(solution)/shard_map/all_gather | solution.py:79
  63.9 1.4 copy.44
  65.3 23.4 %all_to_all.19 = bf16[32,32,512]{2,0,1:T(8,128)(2,1)S(1)} all-to-all(bf16[32,32,512]{2,0,1:T(8,128)(2,1)S(1)} %bitcast.29), channel_id=1, replica_groups=mesh['dp'=32,'tp'=8] {'dp'}, dimensions={1} | all-to-all | bytes 2097152 | tf_op jit(solution)/shard_map/all_to_all | solution.py:80
  88.7 3.2 fusion.32
  91.9 0.0 all-reduce.6.cloned.1.call-start
  91.9 0.6 copy-done.4
  92.6 22.2 %all-gather.3.cloned.1.call-done = bf16[1024,896]{1,0:T(8,128)(2,1)} async-done(((bf16[32,896]{1,0:T(8,128)(2,1)}), bf16[1024,896]{1,0:T(8,128)(2,1)}) %all-gather.3.cloned.1.call-update) | async-done | bytes 1835024 | tf_op jit(solution)/shard_map/all_gather | solution.py:82
  114.7 123.1 %all-reduce.4.cloned.1.call-done = f32[1024,896]{1,0:T(8,128)} async-done(((f32[1024,896]{1,0:T(8,128)}), f32[1024,896]{1,0:T(8,128)}) %all-reduce.4.cloned.1.call-update) | async-done | bytes 3670032 | tf_op jit(solution)/shard_map/psum | solution.py:81
  237.8 4.4 fusion.2
  242.2 17.4 %psum.29 = f32[1024]{0:T(1024)S(1)} all-reduce(f32[1024]{0:T(1024)S(1)} %get-tuple-element.7), channel_id=1, replica_groups=mesh['dp'=32,'tp'=8] {'tp'}, use_global_device_ids=true, to_apply=%region_4.5 | all-reduce | flops 1024 | bytes 8192 | tf_op jit(solution)/shard_map/psum | solution.py:11
  259.7 4.6 fusion.15
  264.3 3.0 fusion.13
  267.3 0.0 reduce-scatter.2.cloned.1.call-start
  267.4 116.9 %all-reduce.6.cloned.1.call-done = (f32[1024,576]{0,1:T(8,128)}, f32[1024,576]{0,1:T(8,128)}) async-done(((f32[1024,576]{0,1:T(8,128)}, f32[1024,576]{0,1:T(8,128)}), (f32[1024,576]{0,1:T(8,128)}, f32[1024,576]{0,1:T(8,128)})) %all-reduce.6.cloned.1.call-update) | async-done | bytes 4718608 | tf_op jit(solution)/shard_map/psum | solution.py:88
  384.3 6.1 %fusion.7 = f32[1024,896]{1,0:T(8,128)} fusion(bf16[576,896]{1,0:T(8,128)(2,1)S(1)} %copy-done.7, f32[1024,576]{0,1:T(8,128)} %get-tuple-element.5, f32[1024,576]{0,1:T(8,128)} %get-tuple-element.6), kind=kOutput, calls=%fused_computation.13 | convolution fusion | flops 1060503552 | bytes 9420800 | tf_op jit(solution)/shard_map/dot_general | solution.py:91
  390.5 87.3 %reduce-scatter.2.cloned.1.call-done = f32[32,896]{1,0:T(8,128)} async-done(((f32[1024,896]{1,0:T(8,128)}), f32[32,896]{1,0:T(8,128)}) %reduce-scatter.2.cloned.1.call-update) | async-done | bytes 114704 | tf_op jit(solution)/shard_map/reduce_scatter | solution.py:90
  477.7 1.5 add_convert_fusion.1
  (34 shorter events, 0.3 us)
Async XLA Ops:
  6.5 3.0 copy-start
  6.5 57.4 %all-gather.5.cloned.1.call-start = ((), (), s32[]{:S(2)}) async-start(), calls=%async_computation.3 | async-start | bytes 1179648 | tf_op jit(solution)/shard_map/all_gather | solution.py:79
  8.0 2.1 copy-start.3
  10.0 6.1 %slice-start = ((s8[9437184]{0:T(1024)(128)(4,1)}), s8[4194304]{0:T(1024)(128)(4,1)S(1)}, s32[]{:S(2)}) async-start(s8[9437184]{0:T(1024)(128)(4,1)} %bitcast.26), calls=%async_computation.7 | async-start | bytes 8388608
  10.4 5.9 %slice-start.1 = ((s8[9437184]{0:T(1024)(128)(4,1)}), s8[4194304]{0:T(1024)(128)(4,1)S(1)}, s32[]{:S(2)}) async-start(s8[9437184]{0:T(1024)(128)(4,1)} %bitcast.26), calls=%async_computation.8 | async-start | bytes 8388608
  10.4 6.1 %slice-start.2 = ((s8[9437184]{0:T(1024)(128)(4,1)}), s8[1048576]{0:T(1024)(128)(4,1)S(1)}, s32[]{:S(2)}) async-start(s8[9437184]{0:T(1024)(128)(4,1)} %bitcast.26), calls=%async_computation.9 | async-start | bytes 2097152
  21.4 67.3 %copy-start.2 = (bf16[512,896]{1,0:T(8,128)(2,1)S(1)}, bf16[512,896]{1,0:T(8,128)(2,1)}, u32[]{:S(2)}) copy-start(bf16[512,896]{1,0:T(8,128)(2,1)} %param.18) | copy-start | bytes 2752516
  22.1 92.6 %all-gather.3.cloned.1.call-start = ((), (), s32[]{:S(2)}) async-start(), calls=%async_computation.2 | async-start | bytes 1892352 | tf_op jit(solution)/shard_map/all_gather | solution.py:82
  22.9 214.9 %all-reduce.4.cloned.1.call-start = ((), (), s32[]{:S(2)}) async-start(), calls=%async_computation.4 | async-start | bytes 7340032 | tf_op jit(solution)/shard_map/psum | solution.py:81
  91.9 0.7 copy-start.4
  91.9 292.4 %all-reduce.6.cloned.1.call-start = ((), (), s32[]{:S(2)}) async-start(), calls=%async_computation.6 | async-start | bytes 9437184 | tf_op jit(solution)/shard_map/psum | solution.py:88
  92.6 167.1 %copy-start.5 = (bf16[896,576]{0,1:T(8,128)(2,1)S(1)}, bf16[896,576]{0,1:T(8,128)(2,1)}, u32[]{:S(2)}) copy-start(bf16[896,576]{0,1:T(8,128)(2,1)} %param.21) | copy-start | bytes 3096580
  259.7 4.6 copy-start.1
  259.7 4.6 copy-start.6
  267.3 117.0 %copy-start.7 = (bf16[576,896]{1,0:T(8,128)(2,1)S(1)}, bf16[576,896]{1,0:T(8,128)(2,1)}, u32[]{:S(2)}) copy-start(bf16[576,896]{1,0:T(8,128)(2,1)} %param.23) | copy-start | bytes 3096580
  267.3 210.4 %reduce-scatter.2.cloned.1.call-start = ((), (), s32[]{:S(2)}) async-start(), calls=%async_computation.5 | async-start | bytes 3784704 | tf_op jit(solution)/shard_map/reduce_scatter | solution.py:90
Sparse Core Ops, SparseCore 0:
  22.2 41.6 all-gather.4
  66.4 48.2 all-gather.2
  118.1 119.6 all-reduce.3
  267.5 116.7 all-reduce.5
  390.6 87.1 reduce-scatter.1
where the time goes:
time: 486 us
  waiting for transfers between devices  391 us (80%)
  blocking collectives  40.9 us (8%)
  matrix products  27.9 us (6%)
  between operations  13.3 us (3%)
  other arithmetic  7.8 us (2%)
    psum x1, waiting for transfers between devices, body(): lax.psum(jnp.dot(blocks, out_proj, preferred_element_type=jnp.float32), '...  123 us
    psum x1, waiting for transfers between devices, body(): gate_act, up_act = lax.psum((gate_part, up_part), 'tp')  117 us
    reduce_scatter x1, waiting for transfers between devices, body(): lax.psum_scatter(jnp.dot(hidden_all, down_weight, preferred_element_type=...  87.3 us
    all_gather x1, waiting for transfers between devices, body(): joined = lax.all_gather(attn_heads, 'tp', axis=1, tiled=True)  41 us
    all_to_all x1, blocking collectives, body(): lax.all_to_all(joined, 'dp', split_axis=1, concat_axis=0, tiled=True)  23.4 us
    all_gather x1, waiting for transfers between devices, body(): residual_all = lax.all_gather(residual, 'dp', axis=0, tiled=True)  22.2 us
    psum x1, blocking collectives, normalize(): square_total = lax.psum(jnp.sum(stream_f * stream_f, axis=1), 'tp')  17.4 us
  transfers between devices with their start and end apart: 5, of which 5 were waited for; matrix products, arithmetic and copies ran while one was open for 1% of the time, Pallas kernels for 0%

commit v1 on v0

v1 whole, which is shorter than its diff:
```python
import jax
import jax.numpy as jnp
from jax import lax
from jax.experimental import pallas as pl
from jax.experimental.pallas import tpu as pltpu
from jax.sharding import PartitionSpec as P

MESH = pl.DeviceIdType.MESH
BF = jnp.bfloat16
F32 = jnp.float32
D = 7168
EPS = 1e-06


def layer_kernel(
    attn, out_proj, residual, gain, gate, up, tails, down,
    out,
    wo, wg, wu, wt, wd, zbuf, ain, proj, rs1, sg, xn, st, stin, rcol, ownf, ownk, p4, z6, hid, dnb, rs2,
    w_l, w_s, w_r, z_s, z_r, a_s, a_r, p_s, p_r, g_s, g_r, t_s, t_r, z6_s, z6_r, h_s, h_r, d_s, d_r,
):
    dp = lax.axis_index("dp")
    k = lax.axis_index("tp")
    c = dp % 2
    p = dp // 2
    x = p // 4

    def chip(q):
        return (2 * q + c, k)

    def level(delta):
        return (dp, (k + 8 + delta) % 8)

    partner = (2 * p + 1 - c, k)

    def remote(src, dst, ssem, rsem, dev):
        return pltpu.make_async_remote_copy(
            src_ref=src, dst_ref=dst, send_sem=ssem, recv_sem=rsem, device_id=dev, device_id_type=MESH
        )

    def arrived(ref, sem):
        pltpu.make_async_copy(ref, ref, sem).wait()

    barrier = pltpu.get_barrier_semaphore()
    pl.semaphore_signal(barrier, inc=1, device_id=partner, device_id_type=MESH)

    def greet_plane(d, _):
        pl.semaphore_signal(barrier, inc=1, device_id=chip((p + d) % 16), device_id_type=MESH)
        return 0

    lax.fori_loop(1, 16, greet_plane, 0)

    def greet_level(d, _):
        pl.semaphore_signal(barrier, inc=1, device_id=level(d), device_id_type=MESH)
        return 0

    lax.fori_loop(1, 8, greet_level, 0)

    main = pl.ds(0, 512)
    d_main = pl.ds(pl.multiple_of(c * 512, 512), 512)
    d_tail = pl.ds(pl.multiple_of(1024 + c * 64, 64), 64)
    pairs = (
        (out_proj, wo.at[c]),
        (gate.at[:, main], wg.at[c]),
        (up.at[:, main], wu.at[c]),
        (tails, wt.at[c]),
        (down.at[main], wd.at[d_main]),
        (down.at[pl.ds(512, 64)], wd.at[d_tail]),
    )
    other_main = pl.ds(pl.multiple_of((1 - c) * 512, 512), 512)
    other_tail = pl.ds(pl.multiple_of(1024 + (1 - c) * 64, 64), 64)
    theirs = (wo.at[1 - c], wg.at[1 - c], wu.at[1 - c], wt.at[1 - c], wd.at[other_main], wd.at[other_tail])
    for n, (src, dst) in enumerate(pairs):
        pltpu.make_async_copy(src, dst, w_l.at[n]).start()

    pl.semaphore_wait(barrier, 23)

    dirs = (1, -1)

    def to_rows(blk, b, ref):
        q = 2 * blk + b

        @pl.when(q != p)
        def _():
            remote(ref, ain.at[p], a_s.at[q], a_r.at[p], chip(q)).start()

        @pl.when(q == p)
        def _():
            pltpu.make_async_copy(ref, ain.at[p], a_r.at[p]).start()

    for b in range(2):
        for di, d in enumerate(dirs):
            remote(attn.at[b], zbuf.at[k, b], z_s.at[di, 0, b], z_r.at[di, 0, b], level(d)).start()
    for n, (src, dst) in enumerate(pairs):
        remote(src, dst, w_s.at[n], w_r.at[n], partner).start()
    for b in range(2):
        to_rows(k, b, attn.at[b])
    for t in range(1, 5):
        for b in range(2):
            for di, d in enumerate(dirs):
                if t == 4 and b != di:
                    continue
                blk = (k + 8 - d * t) % 8
                ref = zbuf.at[blk, b]
                arrived(ref, z_r.at[di, t - 1, b])
                if t < 3 or (t == 3 and b == di):
                    remote(ref, ref, z_s.at[di, t, b], z_r.at[di, t, b], level(d)).start()
                to_rows(blk, b, ref)

    pltpu.make_async_copy(pairs[0][0], pairs[0][1], w_l.at[0]).wait()
    arrived(theirs[0], w_r.at[0])

    def project(g, _):
        first = ((x + 1 + g) % 4) * 4
        for y in range(4):
            arrived(ain.at[first + y], a_r.at[first + y])
        rows = ain[pl.ds(first, 4)].reshape(128, 1024)
        part = jnp.dot(rows, wo[...].reshape(1024, 896), preferred_element_type=F32)
        proj[pl.ds(first, 4)] = part.astype(BF).reshape(4, 32, 896)
        for y in range(4):
            q = first + y

            @pl.when(q != p)
            def _():
                remote(proj.at[q], rs1.at[p], p_s.at[q], p_r.at[p], chip(q)).start()

        return 0

    lax.fori_loop(0, 4, project, 0)

    def add_proj(d, acc):
        q = (p + d) % 16
        arrived(rs1.at[q], p_r.at[q])
        return acc + rs1[q].astype(F32)

    total = residual[...].astype(F32) + proj[p].astype(F32)
    total = lax.fori_loop(1, 16, add_proj, total)
    sg[p] = total.astype(BF)

    def spread(d, _):
        q = (p + d) % 16
        remote(sg.at[p], sg.at[p], g_s.at[q], g_r.at[p], chip(q)).start()
        return 0

    lax.fori_loop(1, 16, spread, 0)

    z6[0, 0, 1] = jnp.zeros((64, 1152), BF)
    z6[1, 0, 0] = jnp.zeros((64, 1152), BF)
    for n in range(1, 6):
        pltpu.make_async_copy(pairs[n][0], pairs[n][1], w_l.at[n]).wait()
        arrived(theirs[n], w_r.at[n])

    def gathered(d, _):
        q = (p + d) % 16
        arrived(sg.at[q], g_r.at[q])
        return 0

    lax.fori_loop(1, 16, gathered, 0)

    gain_f = gain[...].astype(F32)

    def scale(q, _):
        s = sg[pl.ds(4 * q, 4)].reshape(128, 896).astype(F32)
        xn[pl.ds(4 * q, 4)] = (s * gain_f).astype(BF).reshape(4, 32, 896)
        st[q] = lax.dot_general(
            jnp.ones((8, 896), F32),
            s * s,
            (((1,), (1,)), ((), ())),
            precision=lax.Precision.HIGHEST,
            preferred_element_type=F32,
        )
        return 0

    lax.fori_loop(0, 4, scale, 0)

    f = p // 2
    kk = (k + f) % 8

    def send_stat(d, _):
        lab = (kk + d) % 8
        remote(st.at[lab // 2], stin.at[d], t_s.at[d], t_r.at[d], level(d)).start()
        return 0

    lax.fori_loop(1, 8, send_stat, 0)

    def chain(t, _):
        lab_a = (kk + 4 - t + 8) % 8
        lab_b = jnp.where(t == 0, kk, (kk + 4 + t) % 8)
        rows = jnp.concatenate(
            [xn[pl.ds(2 * lab_a, 2)].reshape(64, 896), xn[pl.ds(2 * lab_b, 2)].reshape(64, 896)], axis=0
        )
        for h, w in enumerate((wg, wu)):
            for b in range(2):
                res = jnp.dot(rows, w[b], preferred_element_type=F32)
                ownf[0, h, :, b * 512 : b * 512 + 512] = res[:64]
                ownf[1, h, :, b * 512 : b * 512 + 512] = res[64:]
            res = jnp.dot(rows, wt[h], preferred_element_type=F32)
            ownf[0, h, :, 1024:] = res[:64]
            ownf[1, h, :, 1024:] = res[64:]

        @pl.when(t == 0)
        def _():
            p4[...] = ownf[0].astype(BF)
            for di, d in enumerate(dirs):
                remote(p4.at[di], z6.at[di, 0, di], z6_s.at[di, 0, di], z6_r.at[di, 0, di], level(d)).start()
            ownk[...] = ownf[1]

        @pl.when(t > 0)
        def _():
            for h in range(2):
                for di, d in enumerate(dirs):
                    ref = z6.at[di, t - 1, h]
                    if h == di:
                        arrived(ref, z6_r.at[di, t - 1, h])
                    else:

                        @pl.when(t > 1)
                        def _():
                            arrived(ref, z6_r.at[di, t - 1, h])

                    z6[di, t - 1, h] = (z6[di, t - 1, h].astype(F32) + ownf[di, h]).astype(BF)
                    remote(ref, z6.at[di, t, h], z6_s.at[di, t, h], z6_r.at[di, t, h], level(d)).start()

        return 0

    lax.fori_loop(0, 4, chain, 0)

    def add_stat(d, acc):
        arrived(stin.at[d], t_r.at[d])
        return acc + stin[d]

    square = lax.fori_loop(1, 8, add_stat, st[kk // 2])
    inv = lax.rsqrt(square / D + EPS)
    rcol[...] = jnp.transpose(jnp.broadcast_to(inv[0:1, :], (128, 128)))
    r = rcol[pl.ds(pl.multiple_of((kk % 2) * 64, 64), 64), :][:, 0:1]

    sums = []
    for h in range(2):
        for di in range(2):
            arrived(z6.at[di, 3, h], z6_r.at[di, 3, h])
        sums.append((ownk[h] + z6[0, 3, h].astype(F32) + z6[1, 3, h].astype(F32)) * r)

    def glu(g, u):
        return (g / (1.0 + jnp.exp(-g)) * u).astype(BF)

    t0, t1 = sums[0][:, 1024:], sums[1][:, 1024:]
    low = lax.broadcasted_iota(jnp.int32, (64, 128), 1) < 64
    t0r, t1r = pltpu.roll(t0, 64, 1), pltpu.roll(t1, 64, 1)
    hid[kk, :, :, 0:1024] = glu(sums[0][:, :1024], sums[1][:, :1024]).reshape(2, 32, 1024)
    hid[kk, :, :, 1024:] = glu(jnp.where(low, t0, t1r), jnp.where(low, t0r, t1)).reshape(2, 32, 128)

    for di, d in enumerate(dirs):
        for b in range(2):
            remote(hid.at[kk, b], hid.at[kk, b], h_s.at[di, 0, b], h_r.at[di, 0, b], level(d)).start()

    def lower(labs):
        n = 64 * len(labs)
        rows = [hid[lab].reshape(64, 1152) for lab in labs]
        rows = rows[0] if len(labs) == 1 else jnp.concatenate(rows, axis=0)
        part = jnp.dot(rows, wd[...], preferred_element_type=F32).astype(BF)
        for i, lab in enumerate(labs):
            dnb[pl.ds(2 * lab, 2)] = part[64 * i : 64 * i + 64].reshape(2, 32, 896)
            for b in range(2):
                q = 2 * lab + b

                @pl.when(q != p)
                def _():
                    remote(dnb.at[q], rs2.at[p], d_s.at[q], d_r.at[p], chip(q)).start()

    lower([kk])
    for t in range(1, 5):
        for b in range(2):
            for di, d in enumerate(dirs):
                if t == 4 and b != di:
                    continue
                ref = hid.at[(kk + 8 - d * t) % 8, b]
                arrived(ref, h_r.at[di, t - 1, b])
                if t < 3 or (t == 3 and b == di):
                    remote(ref, ref, h_s.at[di, t, b], h_r.at[di, t, b], level(d)).start()
        if t < 4:
            lower([(kk + 8 - t) % 8, (kk + t) % 8])
        else:
            lower([(kk + 4) % 8])

    def add_down(d, acc):
        q = (p + d) % 16
        arrived(rs2.at[q], d_r.at[q])
        return acc + rs2[q].astype(F32)

    total = sg[p].astype(F32) + dnb[p].astype(F32)
    total = lax.fori_loop(1, 16, add_down, total)
    out[...] = total.astype(BF)

    def sent(ref, sem):
        pltpu.make_async_copy(ref, ref, sem).wait()

    for n in range(6):
        sent(pairs[n][1], w_s.at[n])
    for di in range(2):
        for t in range(4):
            for b in range(2):
                if t < 3 or b == di:
                    sent(zbuf.at[0, 0], z_s.at[di, t, b])
                    sent(hid.at[0, 0], h_s.at[di, t, b])
                if t > 0 or b == di:
                    sent(z6.at[di, 0, 0], z6_s.at[di, t, b])

    def sent_plane(d, _):
        q = (p + d) % 16
        sent(ain.at[q], a_s.at[q])
        sent(proj.at[q], p_s.at[q])
        sent(sg.at[q], g_s.at[q])
        sent(dnb.at[q], d_s.at[q])
        return 0

    lax.fori_loop(1, 16, sent_plane, 0)

    def sent_stat(d, _):
        sent(stin.at[d], t_s.at[d])
        return 0

    lax.fori_loop(1, 8, sent_stat, 0)


def layer(attn, out_proj, residual, gain, gate, up, tails, down):
    vm = pl.BlockSpec(memory_space=pltpu.VMEM)
    hbm = pl.BlockSpec(memory_space=pl.ANY)
    dma = pltpu.SemaphoreType.DMA
    return pl.pallas_call(
        layer_kernel,
        out_shape=jax.ShapeDtypeStruct((32, 896), BF),
        in_specs=[vm, hbm, vm, vm, hbm, hbm, hbm, hbm],
        out_specs=vm,
        scratch_shapes=[
            pltpu.VMEM((2, 512, 896), BF),
            pltpu.VMEM((2, 896, 512), BF),
            pltpu.VMEM((2, 896, 512), BF),
            pltpu.VMEM((2, 896, 128), BF),
            pltpu.VMEM((1152, 896), BF),
            pltpu.VMEM((8, 2, 32, 1024), BF),
            pltpu.VMEM((16, 32, 1024), BF),
            pltpu.VMEM((16, 32, 896), BF),
            pltpu.VMEM((16, 32, 896), BF),
            pltpu.VMEM((16, 32, 896), BF),
            pltpu.VMEM((16, 32, 896), BF),
            pltpu.VMEM((4, 8, 128), F32),
            pltpu.VMEM((8, 8, 128), F32),
            pltpu.VMEM((128, 128), F32),
            pltpu.VMEM((2, 2, 64, 1152), F32),
            pltpu.VMEM((2, 64, 1152), F32),
            pltpu.VMEM((2, 64, 1152), BF),
            pltpu.VMEM((2, 4, 2, 64, 1152), BF),
            pltpu.VMEM((8, 2, 32, 1152), BF),
            pltpu.VMEM((16, 32, 896), BF),
            pltpu.VMEM((16, 32, 896), BF),
            dma((6,)), dma((6,)), dma((6,)),
            dma((2, 4, 2)), dma((2, 4, 2)),
            dma((16,)), dma((16,)),
            dma((16,)), dma((16,)),
            dma((16,)), dma((16,)),
            dma((8,)), dma((8,)),
            dma((2, 4, 2)), dma((2, 4, 2)),
            dma((2, 4, 2)), dma((2, 4, 2)),
            dma((16,)), dma((16,)),
        ],
        compiler_params=pltpu.CompilerParams(
            collective_id=0, has_side_effects=True, vmem_limit_bytes=48 * 2**20
        ),
        name="layer",
    )(attn, out_proj, residual, gain, gate, up, tails, down)


def attention(queries, latent_cache, fresh_latent_entry, lengths, key_up_matrix, value_up_matrix):
    own_rows = queries.shape[0]
    head_count, nope_width, latent_width = key_up_matrix.shape
    rope_width = latent_cache.shape[2] - latent_width
    slot_count = latent_cache.shape[1]
    score_scale = 1.0 / (nope_width + rope_width) ** 0.5
    query_heads = queries.reshape(own_rows, head_count, nope_width + rope_width)
    q_latent = jnp.einsum(
        "rhk,hkl->rhl",
        query_heads[:, :, :nope_width],
        key_up_matrix,
        preferred_element_type=jnp.float32,
    ).astype(jnp.bfloat16)
    q_full = jnp.concatenate([q_latent, query_heads[:, :, nope_width:]], axis=2)
    scores = (
        jnp.einsum("rhc,rjc->rhj", q_full, latent_cache, preferred_element_type=jnp.float32)
        * score_scale
    )
    new_score = (
        jnp.einsum("rhc,rc->rh", q_full, fresh_latent_entry, preferred_element_type=jnp.float32)
        * score_scale
    )
    slot_used = (lax.broadcasted_iota(jnp.int32, (own_rows, slot_count), 1) < lengths[:, None])[
        :, None, :
    ]
    masked = jnp.where(slot_used, scores, -1e30)
    top_score = jnp.maximum(jnp.max(masked, axis=2), new_score)
    weights = jnp.where(slot_used, jnp.exp(masked - top_score[:, :, None]), 0.0)
    new_weight = jnp.exp(new_score - top_score)
    denom = jnp.sum(weights, axis=2) + new_weight
    slot_probabilities = (weights / denom[:, :, None]).astype(jnp.bfloat16)
    fresh_token_prob = (new_weight / denom).astype(jnp.bfloat16)
    latent_result = jnp.einsum(
        "rhj,rjl->rhl",
        slot_probabilities,
        latent_cache[:, :, :latent_width],
        preferred_element_type=jnp.float32,
    )
    latent_result = latent_result + fresh_token_prob.astype(jnp.float32)[
        :, :, None
    ] * fresh_latent_entry[:, None, :latent_width].astype(jnp.float32)
    attn_latent = latent_result.astype(jnp.bfloat16)
    return jnp.einsum(
        "rhl,hlv->rhv", attn_latent, value_up_matrix, preferred_element_type=jnp.float32
    ).astype(jnp.bfloat16)


def body(
    queries,
    latent_cache,
    fresh_latent_entry,
    lengths,
    key_up_matrix,
    value_up_matrix,
    out_proj,
    residual,
    norm_gain,
    gate_weight,
    up_weight,
    down_weight,
):
    tails = jnp.concatenate([gate_weight[:, 512:], up_weight[:, 512:]], axis=1)
    heads = attention(
        queries, latent_cache, fresh_latent_entry, lengths, key_up_matrix, value_up_matrix
    )
    attn = heads.reshape(32, 2, 1024).transpose(1, 0, 2)
    return layer(
        attn, out_proj, residual, norm_gain.reshape(1, -1), gate_weight, up_weight, tails, down_weight
    )


def solution(mesh):
    return jax.shard_map(
        body,
        mesh=mesh,
        in_specs=(
            P("dp", "tp"),
            P("dp", None, None),
            P("dp", None),
            P("dp"),
            P("tp", None, None),
            P("tp", None, None),
            P("dp", "tp"),
            P("dp", "tp"),
            P("tp"),
            P("tp", "dp"),
            P("tp", "dp"),
            P("dp", "tp"),
        ),
        out_specs=P("dp", "tp"),
        check_vma=False,
    )
```

time: 486 us -> 143 us (0.29)
  waiting for transfers between devices: 391 us -> 0 us
  Pallas kernels: 0 us -> 116 us
  blocking collectives: 40.9 us -> 0 us
  matrix products: 27.9 us -> 11 us
  between operations: 13.3 us -> 0.21 us
  local copies, waits for them, and re-layouts: 4.56 us -> 12.5 us
  other arithmetic: 7.8 us -> 1.52 us
    psum x2 -> x0, waiting for transfers between devices: 240 us -> none  [the longest x1 123 us: body(): lax.psum(jnp.dot(blocks, out_proj, preferred_element_type=jnp.float32), '...]
    pallas_call x0 -> x1, Pallas kernels: none -> 116 us  [layer(): pl.pallas_call(layer_kernel, out_shape=jax.ShapeDtypeStruct((32, 896), BF...]
    reduce_scatter x1 -> x0, waiting for transfers between devices: 87.3 us -> none  [body(): lax.psum_scatter(jnp.dot(hidden_all, down_weight, preferred_element_type=...]
    all_gather x2 -> x0, waiting for transfers between devices: 63.1 us -> none  [the longest x1 41 us: body(): joined = lax.all_gather(attn_heads, 'tp', axis=1, tiled=True)]
    all_to_all x1 -> x0, blocking collectives: 23.4 us -> none  [body(): lax.all_to_all(joined, 'dp', split_axis=1, concat_axis=0, tiled=True)]
    psum x1 -> x0, blocking collectives: 17.4 us -> none  [normalize(): square_total = lax.psum(jnp.sum(stream_f * stream_f, axis=1), 'tp')]
    dot_general x9 -> x5, matrix products: 27.9 us -> 11 us  [the longest x1 5.38 us: attention(): jnp.einsum('rhc,rjc->rhj', q_full, latent_cache, preferred_element_type=j...]
    unnamed x23 -> x26, local copies, waits for them, and re-layouts: 1.03 us -> 9.16 us
  transfers between devices with their start and end apart: 5 -> 0, of which waited for: 5 -> 0; matrix products, arithmetic and copies ran while one was open for 1% -> 0% of each run, Pallas kernels for 0% -> 0%
where the time goes in v1:
time: 143 us; the launch traced here: 141 us
  Pallas kernels  116 us (81%)
  local copies, waits for them, and re-layouts  12.5 us (9%)
  matrix products  11 us (8%)
  other arithmetic  1.52 us (1%)
    pallas_call x1, Pallas kernels, layer(): pl.pallas_call(layer_kernel, out_shape=jax.ShapeDtypeStruct((32, 896), BF...  116 us
    unnamed x26, local copies, waits for them, and re-layouts  9.16 us
    dot_general x1, matrix products, attention(): jnp.einsum('rhc,rjc->rhj', q_full, latent_cache, preferred_element_type=j...  5.38 us

profile of v1, /device:TPU:8, one launch (start us, length us, event | category | flops | bytes accessed | tf_op | source)
XLA Modules:
  0.0 141.0 jit_solution(4066378621753954)
XLA Ops:
  0.0 0.0 copy-start
  0.0 1.4 reshape.29
  1.4 0.2 copy-done
  1.7 0.4 fusion.2
  2.2 0.0 slice-start
  2.2 0.1 pad_maximum_fusion
  2.2 0.1 copy-done.7
  2.3 0.1 iota_compare_fusion
  2.4 0.0 slice-start.2
  2.4 5.4 %fusion.22 = (f32[32,16]{1,0:T(8,128)S(1)}, f32[32,16,256]{2,1,0:T(8,128)S(1)}) fusion(bf16[32,256,576]{1,2,0:T(8,128)(2,1)} %param.13, bf16[32,16,576]{2,0,1:T(8,128)(2,1)S(1)} %pad_maximum_fusion, pred[32,256]{1,0:T(8,128)(4,1)S(1)} %iota_compare_fusion), kind=kOutput, calls=%fused_computation.35 | convolution fusion | flops 151387648 | bytes 10561536 | tf_op jit(solution)/shard_map/rhc,rjc->rhj/dot_general | solution.py:387
  7.8 0.0 copy-done.5
  7.8 0.4 fusion.6
  8.2 0.3 fusion.12
  8.5 0.0 slice-done
  8.5 0.0 slice-done.1
  8.5 0.1 slice-done.2
  8.6 2.4 %fusion = f32[32,16,512]{2,1,0:T(8,128)S(1)} fusion(bf16[32,256,576]{1,2,0:T(8,128)(2,1)S(1)} %bitcast.15, f32[32,16,256]{2,1,0:T(8,128)S(1)} %get-tuple-element.8, f32[32,16]{1,0:T(8,128)S(1)} %get-tuple-element.6, f32[32,16]{1,0:T(8,128)S(1)} %multiply_maximum_fusion, pred[32,256]{1,0:T(8,128)(4,1)S(1)} %iota_compare_fusion), kind=kOutput, calls=%fused_computation | convolution fusion | flops 134742016 | bytes 10002432 | tf_op jit(solution)/shard_map/rhj,rjl->rhl/dot_general | solution.py:404
  11.0 0.1 copy.22
  11.1 2.4 %fusion.4 = bf16[32,16,128]{2,0,1:T(8,128)(2,1)S(1)} fusion(bf16[16,512,128]{2,1,0:T(8,128)(2,1)} %param.17, f32[32,16,512]{2,1,0:T(8,128)S(1)} %fusion, f32[32,512]{1,0:T(8,128)S(1)} %slice_convert_fusion, f32[32,16]{0,1:T(8,128)S(1)} %copy.22), kind=kOutput, calls=%fused_computation.7 | convolution fusion | flops 67960832 | bytes 3344384 | tf_op jit(solution)/shard_map/rhl,hlv->rhv/dot_general | solution.py:414
  13.5 0.1 copy.23
  13.7 2.0 %copy.27.gate = bf16[896,576]{1,0:T(8,128)(2,1)S(1)} copy(bf16[896,576]{0,1:T(8,128)(2,1)} %param.21) | data formatting | bytes 2064384 | tf_op args[9]
  15.7 0.0 copy-start.6
  15.7 0.0 copy-start.4
  15.7 0.7 slice.26
  16.5 2.4 %copy.28.up = bf16[896,576]{1,0:T(8,128)(2,1)} copy(bf16[896,576]{0,1:T(8,128)(2,1)} %param.22) | data formatting | bytes 2064384 | tf_op args[10]
  18.8 1.0 slice.27
  19.8 1.1 pad_maximum_fusion.1.tails
  20.9 1.2 copy-done.1
  22.1 1.2 copy-done.2
  23.4 1.2 copy-done.3
  24.5 115.8 %layer.1 = bf16[32,896]{1,0:T(8,128)(2,1)S(1)} custom-call(bf16[2,32,1024]{2,1,0:T(8,128)(2,1)S(1)} %bitcast.13, bf16[512,896]{1,0:T(8,128)(2,1)S(1)} %copy-done.3, bf16[32,896]{1,0:T(8,128)(2,1)S(1)} %copy-done.4, bf16[1,896]{1,0:T(2,128)(2,1)S(1)} %reshape.31.gain, bf16[896,576]{1,0:T(8,128)(2,1)S(1)} %copy.27.gate, bf16[896,576]{1,0:T(8,128)(2,1)S(1)} %copy-done.1, ...), custom_call_target="tpu_custom_call" | custom-call | tf_op jit(solution)/shard_map/layer/pallas_call | solution.py:328
  140.3 0.6 copy.51
  (18 shorter events, 0.2 us)
Async XLA Ops:
  0.0 1.7 %copy-start = (bf16[16,128,512]{2,1,0:T(8,128)(2,1)S(1)}, bf16[16,128,512]{2,1,0:T(8,128)(2,1)}, u32[]{:S(2)}) copy-start(bf16[16,128,512]{2,1,0:T(8,128)(2,1)} %param.16) | copy-start | bytes 6291460
  1.7 0.7 copy-start.7
  2.2 6.3 %slice-start = ((s8[9437184]{0:T(1024)(128)(4,1)}), s8[4194304]{0:T(1024)(128)(4,1)S(1)}, s32[]{:S(2)}) async-start(s8[9437184]{0:T(1024)(128)(4,1)} %bitcast.14), calls=%async_computation | async-start | bytes 8388608
  2.4 5.4 %copy-start.5 = (bf16[32,576]{1,0:T(8,128)(2,1)S(1)}, bf16[32,576]{1,0:T(8,128)(2,1)}, u32[]{:S(2)}) copy-start(bf16[32,576]{1,0:T(8,128)(2,1)} %param.14) | copy-start | bytes 110596
  2.4 6.1 %slice-start.1 = ((s8[9437184]{0:T(1024)(128)(4,1)}), s8[4194304]{0:T(1024)(128)(4,1)S(1)}, s32[]{:S(2)}) async-start(s8[9437184]{0:T(1024)(128)(4,1)} %bitcast.14), calls=%async_computation.1 | async-start | bytes 8388608
  2.4 6.2 %slice-start.2 = ((s8[9437184]{0:T(1024)(128)(4,1)}), s8[1048576]{0:T(1024)(128)(4,1)S(1)}, s32[]{:S(2)}) async-start(s8[9437184]{0:T(1024)(128)(4,1)} %bitcast.14), calls=%async_computation.2 | async-start | bytes 2097152
  15.7 5.1 %copy-start.6 = (bf16[896]{0:T(1024)(128)(2,1)S(1)}, bf16[896]{0:T(1024)(128)(2,1)}, u32[]{:S(2)}) copy-start(bf16[896]{0:T(1024)(128)(2,1)} %param.20) | copy-start | bytes 5380
  15.7 5.1 %copy-start.4 = (bf16[32,896]{1,0:T(8,128)(2,1)S(1)}, bf16[32,896]{1,0:T(8,128)(2,1)}, u32[]{:S(2)}) copy-start(bf16[32,896]{1,0:T(8,128)(2,1)} %residual.1) | copy-start | bytes 172036
  20.9 1.3 copy-start.1
  22.1 1.2 copy-start.2
  23.4 1.2 copy-start.3

commit v2 on v0

v2 whole, which is shorter than its diff:
```python
import jax
import jax.numpy as jnp
from jax import lax
from jax.experimental import pallas as pl
from jax.experimental.pallas import tpu as pltpu
from jax.sharding import PartitionSpec as P

MESH = pl.DeviceIdType.MESH
BF = jnp.bfloat16
F32 = jnp.float32
D = 7168
EPS = 1e-06
GROUP = 8
GROUPS = 4
SCALE = 1.0 / 192**0.5


def layer_kernel(
    lengths, q_full, fresh, cache, value_up, out_proj, residual, gain, gate, up, down,
    out,
    keys, vup, fresh_f, lat, attn, wo, wg, wu, wd, zbuf, ain, proj, rs1, sg, xn, st, stin, rcol, own, p4, z6, hid, dnb, rs2,
    c_s, v_s, w_l, w_s, w_r, z_s, z_r, a_s, a_r, p_s, p_r, g_s, g_r, t_s, t_r, z6_s, z6_r, h_s, h_r, d_s, d_r,
):
    dp = lax.axis_index("dp")
    k = lax.axis_index("tp")
    c = dp % 2
    p = dp // 2

    def chip(q):
        return (2 * q + c, k)

    def level(delta):
        return (dp, (k + 8 + delta) % 8)

    partner = (2 * p + 1 - c, k)
    dirs = (1, -1)
    leaving = []

    def remote(src, dst, ssem, rsem, dev):
        return pltpu.make_async_remote_copy(
            src_ref=src, dst_ref=dst, send_sem=ssem, recv_sem=rsem, device_id=dev, device_id_type=MESH
        )

    def send(src, dst, ssem, rsem, dev):
        remote(src, dst, ssem, rsem, dev).start()
        leaving.append((src, ssem))

    def arrived(ref, sem):
        pltpu.make_async_copy(ref, ref, sem).wait()

    barrier = pltpu.get_barrier_semaphore()
    pl.semaphore_signal(barrier, inc=1, device_id=partner, device_id_type=MESH)

    def greet_plane(d, _):
        pl.semaphore_signal(barrier, inc=1, device_id=chip((p + d) % 16), device_id_type=MESH)
        return 0

    lax.fori_loop(1, 16, greet_plane, 0)

    def greet_level(d, _):
        pl.semaphore_signal(barrier, inc=1, device_id=level(d), device_id_type=MESH)
        return 0

    lax.fori_loop(1, 8, greet_level, 0)

    for g in range(GROUPS):
        rows = pl.ds(g * GROUP, GROUP)
        pltpu.make_async_copy(cache.at[rows], keys.at[rows], c_s.at[g]).start()
        if g == 1:
            pltpu.make_async_copy(value_up, vup, v_s).start()
    pairs = ((out_proj, wo.at[c]), (gate, wg.at[c]), (up, wu.at[c]), (down, wd.at[c]))
    theirs = (wo.at[1 - c], wg.at[1 - c], wu.at[1 - c], wd.at[1 - c])
    for n, (src, dst) in enumerate(pairs):
        pltpu.make_async_copy(src, dst, w_l.at[n]).start()
    fresh_f[...] = fresh[...].astype(F32)

    def weight(n):
        pltpu.make_async_copy(pairs[n][0], pairs[n][1], w_l.at[n]).wait()
        arrived(theirs[n], w_r.at[n])

    slot = lax.broadcasted_iota(jnp.int32, (16, 256), 1)

    def attend(g):
        arrived(keys.at[pl.ds(g * GROUP, GROUP)], c_s.at[g])
        scores, new_score, used = [], [], []
        for i in range(GROUP):
            r = g * GROUP + i
            q = q_full[r]
            entry = fresh_f[pl.ds(r, 1), :]
            scores.append(jnp.dot(q, keys[r], preferred_element_type=F32) * SCALE)
            new_score.append(jnp.sum(q.astype(F32) * entry, axis=1, keepdims=True) * SCALE)
            used.append(slot < lengths[r])
        masked = jnp.concatenate([jnp.where(u, v, -1e30) for u, v in zip(used, scores)], axis=0)
        new_score = jnp.concatenate(new_score, axis=0)
        top = jnp.maximum(jnp.max(masked, axis=1, keepdims=True), new_score)
        powers = jnp.exp(masked - top)
        weights = jnp.concatenate(
            [jnp.where(u, powers[16 * i : 16 * i + 16], 0.0) for i, u in enumerate(used)], axis=0
        )
        new_weight = jnp.exp(new_score - top)
        denom = jnp.sum(weights, axis=1, keepdims=True) + new_weight
        probs = (weights / denom).astype(BF)
        new_prob = (new_weight / denom).astype(BF).astype(F32)
        for i in range(GROUP):
            r = g * GROUP + i
            own_rows = slice(16 * i, 16 * i + 16)
            res = lax.dot_general(
                probs[own_rows], keys[r, 0:512, :], (((1,), (1,)), ((), ())), preferred_element_type=F32
            )
            lat[:, r % 16, :] = res + new_prob[own_rows] * fresh_f[pl.ds(r, 1), 0:512]

    def attend_groups(first, last):
        lax.fori_loop(first, last, lambda g, _: (attend(g), 0)[1], 0)

    def heads_out(ch):
        def head(h, _):
            res = jnp.dot(lat[h].astype(BF), vup[h], preferred_element_type=F32)
            attn[h // 8, ch, :, pl.ds(pl.multiple_of((h % 8) * 128, 128), 128)] = res.astype(BF)
            return 0

        lax.fori_loop(0, 16, head, 0, unroll=4)

    def to_rows(blk, b, ch, ref):
        q = 2 * blk + b

        @pl.when(q != p)
        def _():
            remote(ref, ain.at[ch, p], a_s.at[ch, q], a_r.at[ch, p], chip(q)).start()

        @pl.when(q == p)
        def _():
            pltpu.make_async_copy(ref, ain.at[ch, p], a_r.at[ch, p]).start()

    def heads_start(ch):
        for b in range(2):
            for di, d in enumerate(dirs):
                send(attn.at[b, ch], zbuf.at[k, b, ch], z_s.at[ch, di, 0, b], z_r.at[ch, di, 0, b], level(d))
        for b in range(2):
            to_rows(k, b, ch, attn.at[b, ch])

    def heads_step(ch, t):
        for b in range(2):
            for di, d in enumerate(dirs):
                if t == 4 and b != di:
                    continue
                blk = (k + 8 - d * t) % 8
                ref = zbuf.at[blk, b, ch]
                arrived(ref, z_r.at[ch, di, t - 1, b])
                if t < 3 or (t == 3 and b == di):
                    send(ref, ref, z_s.at[ch, di, t, b], z_r.at[ch, di, t, b], level(d))
                to_rows(blk, b, ch, ref)

    def swap():
        pl.semaphore_wait(barrier, 23)
        for n, (src, dst) in enumerate(pairs):
            send(src, dst, w_s.at[n], w_r.at[n], partner)

    def project(ch, send_now):
        def group(g, _):
            first = (((p // 8) + 1 + g) % 2) * 8

            def wait_rows(j, _):
                arrived(ain.at[ch, first + j], a_r.at[ch, first + j])
                return 0

            lax.fori_loop(0, 8, wait_rows, 0)
            rows = ain[ch, pl.ds(first, 8)].reshape(128, 1024)
            part = jnp.dot(rows, wo[...].reshape(1024, 896), preferred_element_type=F32)
            proj[ch, pl.ds(first, 8)] = part.astype(BF).reshape(8, 16, 896)
            if send_now:
                for j in range(8):

                    @pl.when(first + j != p)
                    def _():
                        q = first + j
                        remote(proj.at[ch, q], rs1.at[ch, p], p_s.at[ch, q], p_r.at[ch, p], chip(q)).start()

            return 0

        lax.fori_loop(0, 2, group, 0)

    def send_proj(ch):
        def one(d, _):
            q = (p + d) % 16
            remote(proj.at[ch, q], rs1.at[ch, p], p_s.at[ch, q], p_r.at[ch, p], chip(q)).start()
            return 0

        lax.fori_loop(1, 16, one, 0)

    def join(ch):
        def add(d, acc):
            q = (p + d) % 16
            arrived(rs1.at[ch, q], p_r.at[ch, q])
            return acc + rs1[ch, q].astype(F32)

        total = residual[16 * ch : 16 * ch + 16].astype(F32) + proj[ch, p].astype(F32)
        sg[ch, p] = lax.fori_loop(1, 16, add, total).astype(BF)

        def spread(d, _):
            q = (p + d) % 16
            remote(sg.at[ch, p], sg.at[ch, p], g_s.at[ch, q], g_r.at[ch, p], chip(q)).start()
            return 0

        lax.fori_loop(1, 16, spread, 0)

    f = p // 2
    kk = (k + f) % 8

    def lab(delta):
        return (kk + 8 + delta) % 8

    def expand(ch):
        def gathered(d, _):
            q = (p + d) % 16
            arrived(sg.at[ch, q], g_r.at[ch, q])
            return 0

        lax.fori_loop(1, 16, gathered, 0)
        gain_f = gain[...].astype(F32)

        def scale(g, _):
            s = sg[ch, pl.ds(8 * g, 8)].reshape(128, 896).astype(F32)
            xn[ch, pl.ds(8 * g, 8)] = (s * gain_f).astype(BF).reshape(8, 16, 896)
            sq = s * s
            lanes = sq[:, 0:128]
            for i in range(1, 7):
                lanes = lanes + sq[:, 128 * i : 128 * i + 128]
            st[ch, g] = jnp.broadcast_to(jnp.sum(jnp.transpose(lanes), axis=0, keepdims=True), (8, 128))
            return 0

        lax.fori_loop(0, 2, scale, 0)
        rows = xn[ch].reshape(256, 896)
        for h, w in enumerate((wg, wu)):
            res = lax.dot_general(
                rows, w[...].reshape(1152, 896), (((1,), (1,)), ((), ())), preferred_element_type=F32
            )
            own[ch, h] = res.reshape(8, 32, 1152)
            p4[ch, h] = own[ch, h, lab(4)].astype(BF)
            send(
                p4.at[ch, h], z6.at[ch, h, 0, h], z6_s.at[ch, h, 0, h], z6_r.at[ch, h, 0, h], level(dirs[h])
            )

        def send_stat(d, _):
            remote(
                st.at[ch, lab(d) // 4], stin.at[ch, d], t_s.at[ch, d], t_r.at[ch, d], level(d)
            ).start()
            return 0

        lax.fori_loop(1, 8, send_stat, 0)

    def chain(ch, t):
        for h in range(2):
            for di, d in enumerate(dirs):
                ref = z6.at[ch, di, t - 1, h]
                mine = own[ch, h, lab(d * (4 - t))]
                if h == di or t > 1:
                    arrived(ref, z6_r.at[ch, di, t - 1, h])
                    mine = mine + z6[ch, di, t - 1, h].astype(F32)
                z6[ch, di, t - 1, h] = mine.astype(BF)
                send(ref, z6.at[ch, di, t, h], z6_s.at[ch, di, t, h], z6_r.at[ch, di, t, h], level(d))

    def lower(ch, labs):
        n = 32 * len(labs)
        rows = [hid[ch, l].reshape(32, 1152) for l in labs]
        rows = rows[0] if len(labs) == 1 else jnp.concatenate(rows, axis=0)
        part = jnp.dot(rows, wd[...].reshape(1152, 896), preferred_element_type=F32).astype(BF)
        for i, l in enumerate(labs):
            dnb[ch, pl.ds(2 * l, 2)] = part[32 * i : 32 * i + 32].reshape(2, 16, 896)
            for b in range(2):
                q = 2 * l + b

                @pl.when(q != p)
                def _():
                    remote(dnb.at[ch, q], rs2.at[ch, p], d_s.at[ch, q], d_r.at[ch, p], chip(q)).start()

    def activate(ch):
        def add_stat(d, acc):
            arrived(stin.at[ch, d], t_r.at[ch, d])
            return acc + stin[ch, d]

        square = lax.fori_loop(1, 8, add_stat, st[ch, kk // 4])
        inv = lax.rsqrt(square / D + EPS)
        rcol[ch] = jnp.transpose(jnp.broadcast_to(inv[0:1, :], (128, 128)))
        r = rcol[ch, pl.ds(pl.multiple_of((kk % 4) * 32, 32), 32), :][:, 0:1]
        sums = []
        for h in range(2):
            for di in range(2):
                arrived(z6.at[ch, di, 3, h], z6_r.at[ch, di, 3, h])
            total = own[ch, h, kk] + z6[ch, 0, 3, h].astype(F32) + z6[ch, 1, 3, h].astype(F32)
            sums.append(total * r)
        units = sums[0] / (1.0 + jnp.exp(-sums[0])) * sums[1]
        hid[ch, kk] = units.astype(BF).reshape(2, 16, 1152)
        for di, d in enumerate(dirs):
            for b in range(2):
                ref = hid.at[ch, kk, b]
                send(ref, ref, h_s.at[ch, di, 0, b], h_r.at[ch, di, 0, b], level(d))

    def collect(ch, t):
        for b in range(2):
            for di, d in enumerate(dirs):
                if t == 4 and b != di:
                    continue
                ref = hid.at[ch, lab(-d * t), b]
                arrived(ref, h_r.at[ch, di, t - 1, b])
                if t < 3 or (t == 3 and b == di):
                    send(ref, ref, h_s.at[ch, di, t, b], h_r.at[ch, di, t, b], level(d))

    def finish(ch):
        def add(d, acc):
            q = (p + d) % 16
            arrived(rs2.at[ch, q], d_r.at[ch, q])
            return acc + rs2[ch, q].astype(F32)

        total = sg[ch, p].astype(F32) + dnb[ch, p].astype(F32)
        out[16 * ch : 16 * ch + 16] = lax.fori_loop(1, 16, add, total).astype(BF)

    attend_groups(0, 1)
    swap()
    attend_groups(1, 2)
    pltpu.make_async_copy(value_up, vup, v_s).wait()
    heads_out(0)
    heads_start(0)
    attend_groups(2, 3)
    heads_step(0, 1)
    attend_groups(3, 4)
    heads_step(0, 2)
    heads_out(1)
    heads_start(1)
    heads_step(0, 3)
    heads_step(1, 1)
    heads_step(0, 4)
    heads_step(1, 2)
    weight(0)
    heads_step(1, 3)
    project(0, True)
    heads_step(1, 4)
    project(1, False)
    join(0)
    send_proj(1)
    weight(1)
    weight(2)
    expand(0)
    chain(0, 1)
    join(1)
    chain(0, 2)
    chain(0, 3)
    expand(1)
    chain(1, 1)
    activate(0)
    chain(1, 2)
    weight(3)
    collect(0, 1)
    lower(0, [kk])
    chain(1, 3)
    collect(0, 2)
    lower(0, [lab(1), lab(-1)])
    activate(1)
    collect(0, 3)
    lower(0, [lab(2), lab(-2)])
    collect(1, 1)
    lower(1, [kk])
    collect(0, 4)
    lower(0, [lab(3), lab(-3)])
    collect(1, 2)
    lower(0, [lab(4)])
    lower(1, [lab(1), lab(-1)])
    collect(1, 3)
    lower(1, [lab(2), lab(-2)])
    collect(1, 4)
    lower(1, [lab(3), lab(-3)])
    lower(1, [lab(4)])
    finish(0)
    finish(1)

    for ref, sem in leaving:
        pltpu.make_async_copy(ref, ref, sem).wait()

    def sent_plane(d, _):
        q = (p + d) % 16
        for ch in range(2):
            for ref, sem in ((ain, a_s), (proj, p_s), (sg, g_s), (dnb, d_s)):
                pltpu.make_async_copy(ref.at[ch, q], ref.at[ch, q], sem.at[ch, q]).wait()
        return 0

    lax.fori_loop(1, 16, sent_plane, 0)

    def sent_stat(d, _):
        for ch in range(2):
            pltpu.make_async_copy(stin.at[ch, d], stin.at[ch, d], t_s.at[ch, d]).wait()
        return 0

    lax.fori_loop(1, 8, sent_stat, 0)


def layer(lengths, q_full, fresh, cache, value_up, out_proj, residual, gain, gate, up, down):
    vm = pl.BlockSpec(memory_space=pltpu.VMEM)
    hbm = pl.BlockSpec(memory_space=pl.ANY)
    dma = pltpu.SemaphoreType.DMA
    plane = pltpu.VMEM((2, 16, 16, 896), BF)
    return pl.pallas_call(
        layer_kernel,
        out_shape=jax.ShapeDtypeStruct((32, 896), BF),
        in_specs=[pl.BlockSpec(memory_space=pltpu.SMEM), vm, vm, hbm, hbm, hbm, vm, vm, hbm, hbm, hbm],
        out_specs=vm,
        scratch_shapes=[
            pltpu.VMEM((32, 576, 256), BF),
            pltpu.VMEM((16, 512, 128), BF),
            pltpu.VMEM((32, 576), F32),
            pltpu.VMEM((16, 16, 512), F32),
            pltpu.VMEM((2, 2, 16, 1024), BF),
            pltpu.VMEM((2, 512, 896), BF),
            pltpu.VMEM((2, 576, 896), BF),
            pltpu.VMEM((2, 576, 896), BF),
            pltpu.VMEM((2, 576, 896), BF),
            pltpu.VMEM((8, 2, 2, 16, 1024), BF),
            pltpu.VMEM((2, 16, 16, 1024), BF),
            plane, plane, plane, plane,
            pltpu.VMEM((2, 2, 8, 128), F32),
            pltpu.VMEM((2, 8, 8, 128), F32),
            pltpu.VMEM((2, 128, 128), F32),
            pltpu.VMEM((2, 2, 8, 32, 1152), F32),
            pltpu.VMEM((2, 2, 32, 1152), BF),
            pltpu.VMEM((2, 2, 4, 2, 32, 1152), BF),
            pltpu.VMEM((2, 8, 2, 16, 1152), BF),
            plane, plane,
            dma((GROUPS,)), dma,
            dma((4,)), dma((4,)), dma((4,)),
            dma((2, 2, 4, 2)), dma((2, 2, 4, 2)),
            dma((2, 16)), dma((2, 16)),
            dma((2, 16)), dma((2, 16)),
            dma((2, 16)), dma((2, 16)),
            dma((2, 8)), dma((2, 8)),
            dma((2, 2, 4, 2)), dma((2, 2, 4, 2)),
            dma((2, 2, 4, 2)), dma((2, 2, 4, 2)),
            dma((2, 16)), dma((2, 16)),
        ],
        compiler_params=pltpu.CompilerParams(
            collective_id=0, has_side_effects=True, vmem_limit_bytes=56 * 2**20
        ),
        name="layer",
    )(lengths, q_full, fresh, cache, value_up, out_proj, residual, gain, gate, up, down)


def body(
    queries,
    latent_cache,
    fresh_latent_entry,
    lengths,
    key_up_matrix,
    value_up_matrix,
    out_proj,
    residual,
    norm_gain,
    gate_weight,
    up_weight,
    down_weight,
):
    query_heads = queries.reshape(32, 16, 192)
    q_latent = jnp.einsum(
        "rhk,hkl->rhl", query_heads[:, :, :128], key_up_matrix, preferred_element_type=F32
    ).astype(BF)
    q_full = jnp.concatenate([q_latent, query_heads[:, :, 128:]], axis=2)
    return layer(
        lengths,
        q_full,
        fresh_latent_entry,
        latent_cache.transpose(0, 2, 1),
        value_up_matrix,
        out_proj,
        residual,
        norm_gain.reshape(1, -1),
        gate_weight.T,
        up_weight.T,
        down_weight,
    )


def solution(mesh):
    return jax.shard_map(
        body,
        mesh=mesh,
        in_specs=(
            P("dp", "tp"),
            P("dp", None, None),
            P("dp", None),
            P("dp"),
            P("tp", None, None),
            P("tp", None, None),
            P("dp", "tp"),
            P("dp", "tp"),
            P("tp"),
            P("tp", "dp"),
            P("tp", "dp"),
            P("dp", "tp"),
        ),
        out_specs=P("dp", "tp"),
        check_vma=False,
    )
```

time: 486 us -> 125 us (0.26)
  waiting for transfers between devices: 391 us -> 0 us
  Pallas kernels: 0 us -> 119 us
  blocking collectives: 40.9 us -> 0 us
  matrix products: 27.9 us -> 0.39 us
  between operations: 13.3 us -> 0.05 us
  other arithmetic: 7.8 us -> 0.9 us
    psum x2 -> x0, waiting for transfers between devices: 240 us -> none  [the longest x1 123 us: body(): lax.psum(jnp.dot(blocks, out_proj, preferred_element_type=jnp.float32), '...]
    pallas_call x0 -> x1, Pallas kernels: none -> 119 us  [layer(): pl.pallas_call(layer_kernel, out_shape=jax.ShapeDtypeStruct((32, 896), BF...]
    reduce_scatter x1 -> x0, waiting for transfers between devices: 87.3 us -> none  [body(): lax.psum_scatter(jnp.dot(hidden_all, down_weight, preferred_element_type=...]
    all_gather x2 -> x0, waiting for transfers between devices: 63.1 us -> none  [the longest x1 41 us: body(): joined = lax.all_gather(attn_heads, 'tp', axis=1, tiled=True)]
    dot_general x9 -> x1, matrix products: 27.9 us -> 0.39 us  [body(): jnp.einsum('rhk,hkl->rhl', query_heads[:, :, :128], key_up_matrix, prefer...]
    all_to_all x1 -> x0, blocking collectives: 23.4 us -> none  [body(): lax.all_to_all(joined, 'dp', split_axis=1, concat_axis=0, tiled=True)]
    psum x1 -> x0, blocking collectives: 17.4 us -> none  [normalize(): square_total = lax.psum(jnp.sum(stream_f * stream_f, axis=1), 'tp')]
  transfers between devices with their start and end apart: 5 -> 0, of which waited for: 5 -> 0; matrix products, arithmetic and copies ran while one was open for 1% -> 0% of each run, Pallas kernels for 0% -> 0%
where the time goes in v2:
time: 125 us; the launch traced here: 124 us
  Pallas kernels  119 us (95%)
  local copies, waits for them, and re-layouts  4.02 us (3%)
    pallas_call x1, Pallas kernels, layer(): pl.pallas_call(layer_kernel, out_shape=jax.ShapeDtypeStruct((32, 896), BF...  119 us

profile of v2, /device:TPU:8, one launch (start us, length us, event | category | flops | bytes accessed | tf_op | source)
XLA Modules:
  0.0 124.2 jit_solution(16107627538425148171)
XLA Ops:
  0.0 0.0 copy-start
  0.0 1.4 %reshape.6 = bf16[32,16,192]{2,1,0:T(8,128)(2,1)S(1)} reshape(bf16[32,3072]{1,0:T(8,128)(2,1)} %param.12) | data formatting | bytes 393216 | tf_op jit(solution)/shard_map/reshape | solution.py:458
  1.4 0.2 copy-done
  1.7 0.0 copy-start.1
  1.7 0.4 fusion.1
  2.1 0.3 copy.20
  2.4 0.9 pad_maximum_fusion.q_full
  3.3 0.0 copy-done.1
  3.3 0.6 reshape.7.gain
  3.9 118.8 %layer.1 = bf16[32,896]{1,0:T(8,128)(2,1)} custom-call(s32[32]{0:T(128)} %lengths.1, bf16[32,16,576]{2,1,0:T(8,128)(2,1)} %pad_maximum_fusion.q_full, bf16[32,576]{1,0:T(8,128)(2,1)} %fresh.1, bf16[32,576,256]{2,1,0:T(8,128)(2,1)} %bitcast.7, bf16[16,512,128]{2,1,0:T(8,128)(2,1)} %value_up.1, bf16[512,896]{1,0:T(8,128)(2,1)} %out_proj.1, ...), custom_call_target="tpu_custom_call" | custom-call | tf_op jit(solution)/shard_map/layer/pallas_call | solution.py:400
  122.7 1.4 %copy.22 = bf16[32,896]{1,0:T(8,128)(2,1)} copy(bf16[32,896]{1,0:T(8,128)(2,1)} %layer.1) | data formatting | bytes 114688
  (2 shorter events, 0.0 us)
Async XLA Ops:
  0.0 1.7 %copy-start = (bf16[16,128,512]{2,1,0:T(8,128)(2,1)S(1)}, bf16[16,128,512]{2,1,0:T(8,128)(2,1)}, u32[]{:S(2)}) copy-start(bf16[16,128,512]{2,1,0:T(8,128)(2,1)} %param.16) | copy-start | bytes 6291460
  1.7 1.6 %copy-start.1 = (bf16[896]{0:T(1024)(128)(2,1)S(1)}, bf16[896]{0:T(1024)(128)(2,1)}, u32[]{:S(2)}) copy-start(bf16[896]{0:T(1024)(128)(2,1)} %param.20) | copy-start | bytes 5380

commit v3 on v2

--- a/solution.py
+++ b/solution.py
@@ -132,23 +132,44 @@
             pltpu.make_async_copy(ref, ain.at[ch, p], a_r.at[ch, p]).start()
 
     def heads_start(ch):
+        for hop in (2, 1):
+            for b in range(2):
+                for di, d in enumerate(dirs):
+                    send(
+                        attn.at[b, ch], zbuf.at[k, b, ch],
+                        z_s.at[ch, di, hop - 1, b], z_r.at[ch, di, hop - 1, b], level(hop * d),
+                    )
+        for b in range(2):
+            to_rows(k, b, ch, attn.at[b, ch])
+
+    def heads_mid(ch):
         for b in range(2):
             for di, d in enumerate(dirs):
-                send(attn.at[b, ch], zbuf.at[k, b, ch], z_s.at[ch, di, 0, b], z_r.at[ch, di, 0, b], level(d))
-        for b in range(2):
-            to_rows(k, b, ch, attn.at[b, ch])
-
-    def heads_step(ch, t):
-        for b in range(2):
-            for di, d in enumerate(dirs):
-                if t == 4 and b != di:
-                    continue
-                blk = (k + 8 - d * t) % 8
+                blk = (k + 8 - 2 * d) % 8
                 ref = zbuf.at[blk, b, ch]
-                arrived(ref, z_r.at[ch, di, t - 1, b])
-                if t < 3 or (t == 3 and b == di):
-                    send(ref, ref, z_s.at[ch, di, t, b], z_r.at[ch, di, t, b], level(d))
-                to_rows(blk, b, ch, ref)
+                arrived(ref, z_r.at[ch, di, 1, b])
+                send(ref, ref, z_s.at[ch, di, 2, b], z_r.at[ch, di, 2, b], level(d))
+                if b == di:
+                    send(ref, ref, z_s.at[ch, di, 3, b], z_r.at[ch, di, 3, b], level(2 * d))
+        for hop in (2, 1):
+            for b in range(2):
+                for di, d in enumerate(dirs):
+                    blk = (k + 8 - hop * d) % 8
+                    ref = zbuf.at[blk, b, ch]
+                    if hop == 1:
+                        arrived(ref, z_r.at[ch, di, 0, b])
+                    to_rows(blk, b, ch, ref)
+
+    def heads_end(ch):
+        for hop in (3, 4):
+            for b in range(2):
+                for di, d in enumerate(dirs):
+                    if hop == 4 and b != di:
+                        continue
+                    blk = (k + 8 - hop * d) % 8
+                    ref = zbuf.at[blk, b, ch]
+                    arrived(ref, z_r.at[ch, di, hop - 1, b])
+                    to_rows(blk, b, ch, ref)
 
     def swap():
         pl.semaphore_wait(barrier, 23)
@@ -216,7 +237,7 @@
             return 0
 
         lax.fori_loop(1, 16, gathered, 0)
-        gain_f = gain[...].astype(F32)
+        gain_f = gain[...].astype(F32).reshape(1, 896)
 
         def scale(g, _):
             s = sg[ch, pl.ds(8 * g, 8)].reshape(128, 896).astype(F32)
@@ -279,6 +300,12 @@
             return acc + stin[ch, d]
 
         square = lax.fori_loop(1, 8, add_stat, st[ch, kk // 4])
+
+        def sent_stat(d, _):
+            pltpu.make_async_copy(stin.at[ch, d], stin.at[ch, d], t_s.at[ch, d]).wait()
+            return 0
+
+        lax.fori_loop(1, 8, sent_stat, 0)
         inv = lax.rsqrt(square / D + EPS)
         rcol[ch] = jnp.transpose(jnp.broadcast_to(inv[0:1, :], (128, 128)))
         r = rcol[ch, pl.ds(pl.multiple_of((kk % 4) * 32, 32), 32), :][:, 0:1]
@@ -290,20 +317,45 @@
             sums.append(total * r)
         units = sums[0] / (1.0 + jnp.exp(-sums[0])) * sums[1]
         hid[ch, kk] = units.astype(BF).reshape(2, 16, 1152)
-        for di, d in enumerate(dirs):
-            for b in range(2):
-                ref = hid.at[ch, kk, b]
-                send(ref, ref, h_s.at[ch, di, 0, b], h_r.at[ch, di, 0, b], level(d))
-
-    def collect(ch, t):
+        for hop in (2, 1):
+            for di, d in enumerate(dirs):
+                for b in range(2):
+                    ref = hid.at[ch, kk, b]
+                    send(ref, ref, h_s.at[ch, di, hop - 1, b], h_r.at[ch, di, hop - 1, b], level(hop * d))
+
+    def collect_mid(ch):
         for b in range(2):
             for di, d in enumerate(dirs):
-                if t == 4 and b != di:
-                    continue
-                ref = hid.at[ch, lab(-d * t), b]
-                arrived(ref, h_r.at[ch, di, t - 1, b])
-                if t < 3 or (t == 3 and b == di):
-                    send(ref, ref, h_s.at[ch, di, t, b], h_r.at[ch, di, t, b], level(d))
+                ref = hid.at[ch, lab(-2 * d), b]
+                arrived(ref, h_r.at[ch, di, 1, b])
+                send(ref, ref, h_s.at[ch, di, 2, b], h_r.at[ch, di, 2, b], level(d))
+                if b == di:
+                    send(ref, ref, h_s.at[ch, di, 3, b], h_r.at[ch, di, 3, b], level(2 * d))
+        for b in range(2):
+            for di, d in enumerate(dirs):
+                arrived(hid.at[ch, lab(-d), b], h_r.at[ch, di, 0, b])
+
+    def collect_end(ch):
+        for hop in (3, 4):
+            for b in range(2):
+                for di, d in enumerate(dirs):
+                    if hop == 3 or b == di:
+                        arrived(hid.at[ch, lab(-hop * d), b], h_r.at[ch, di, hop - 1, b])
+
+    def settle(kinds, chunks):
+        def one(d, _):
+            q = (p + d) % 16
+            for ch in chunks:
+                for ref, sem in kinds:
+                    pltpu.make_async_copy(ref.at[ch, q], ref.at[ch, q], sem.at[ch, q]).wait()
+            return 0
+
+        lax.fori_loop(1, 16, one, 0)
+
+    def settle_all():
+        for ref, sem in leaving:
+            pltpu.make_async_copy(ref, ref, sem).wait()
+        leaving.clear()
 
     def finish(ch):
         def add(d, acc):
@@ -320,76 +372,49 @@
     pltpu.make_async_copy(value_up, vup, v_s).wait()
     heads_out(0)
     heads_start(0)
-    attend_groups(2, 3)
-    heads_step(0, 1)
-    attend_groups(3, 4)
-    heads_step(0, 2)
+    attend_groups(2, 4)
+    heads_mid(0)
     heads_out(1)
     heads_start(1)
-    heads_step(0, 3)
-    heads_step(1, 1)
-    heads_step(0, 4)
-    heads_step(1, 2)
     weight(0)
-    heads_step(1, 3)
+    heads_end(0)
+    heads_mid(1)
     project(0, True)
-    heads_step(1, 4)
+    heads_end(1)
     project(1, False)
     join(0)
     send_proj(1)
     weight(1)
     weight(2)
     expand(0)
+    join(1)
     chain(0, 1)
-    join(1)
     chain(0, 2)
+    expand(1)
     chain(0, 3)
-    expand(1)
     chain(1, 1)
     activate(0)
     chain(1, 2)
     weight(3)
-    collect(0, 1)
     lower(0, [kk])
+    settle(((ain, a_s), (proj, p_s), (sg, g_s)), (0, 1))
+    collect_mid(0)
     chain(1, 3)
-    collect(0, 2)
-    lower(0, [lab(1), lab(-1)])
+    lower(0, [lab(1), lab(-1), lab(2), lab(-2)])
+    collect_end(0)
     activate(1)
-    collect(0, 3)
-    lower(0, [lab(2), lab(-2)])
-    collect(1, 1)
+    lower(0, [lab(3), lab(-3), lab(4)])
     lower(1, [kk])
-    collect(0, 4)
-    lower(0, [lab(3), lab(-3)])
-    collect(1, 2)
-    lower(0, [lab(4)])
-    lower(1, [lab(1), lab(-1)])
-    collect(1, 3)
-    lower(1, [lab(2), lab(-2)])
-    collect(1, 4)
-    lower(1, [lab(3), lab(-3)])
-    lower(1, [lab(4)])
+    settle_all()
+    collect_mid(1)
+    lower(1, [lab(1), lab(-1), lab(2), lab(-2)])
+    settle(((dnb, d_s),), (0,))
     finish(0)
+    collect_end(1)
+    lower(1, [lab(3), lab(-3), lab(4)])
+    settle_all()
     finish(1)
-
-    for ref, sem in leaving:
-        pltpu.make_async_copy(ref, ref, sem).wait()
-
-    def sent_plane(d, _):
-        q = (p + d) % 16
-        for ch in range(2):
-            for ref, sem in ((ain, a_s), (proj, p_s), (sg, g_s), (dnb, d_s)):
-                pltpu.make_async_copy(ref.at[ch, q], ref.at[ch, q], sem.at[ch, q]).wait()
-        return 0
-
-    lax.fori_loop(1, 16, sent_plane, 0)
-
-    def sent_stat(d, _):
-        for ch in range(2):
-            pltpu.make_async_copy(stin.at[ch, d], stin.at[ch, d], t_s.at[ch, d]).wait()
-        return 0
-
-    lax.fori_loop(1, 8, sent_stat, 0)
+    settle(((dnb, d_s),), (1,))
 
 
 def layer(lengths, q_full, fresh, cache, value_up, out_proj, residual, gain, gate, up, down):
@@ -435,7 +460,7 @@
             dma((2, 16)), dma((2, 16)),
         ],
         compiler_params=pltpu.CompilerParams(
-            collective_id=0, has_side_effects=True, vmem_limit_bytes=56 * 2**20
+            collective_id=0, has_side_effects=True, vmem_limit_bytes=53 * 2**20
         ),
         name="layer",
     )(lengths, q_full, fresh, cache, value_up, out_proj, residual, gain, gate, up, down)
@@ -468,7 +493,7 @@
         value_up_matrix,
         out_proj,
         residual,
-        norm_gain.reshape(1, -1),
+        norm_gain,
         gate_weight.T,
         up_weight.T,
         down_weight,

time: 125 us -> 115 us (0.920)
  Pallas kernels: 119 us -> 112 us
  local copies, waits for them, and re-layouts: 4.02 us -> 2.63 us
    pallas_call x1, Pallas kernels: 119 us -> 112 us  [layer(): pl.pallas_call(layer_kernel, out_shape=jax.ShapeDtypeStruct((32, 896), BF...]
where the time goes in v3:
time: 115 us
  Pallas kernels  112 us (97%)
  local copies, waits for them, and re-layouts  2.63 us (2%)
    pallas_call x1, Pallas kernels, layer(): pl.pallas_call(layer_kernel, out_shape=jax.ShapeDtypeStruct((32, 896), BF...  112 us

profile of v3, /device:TPU:8, one launch (start us, length us, event | category | flops | bytes accessed | tf_op | source)
XLA Modules:
  0.0 114.7 jit_solution(5068690061364375816)
XLA Ops:
  0.0 0.0 copy-start
  0.0 1.4 %reshape.3 = bf16[32,16,192]{2,1,0:T(8,128)(2,1)S(1)} reshape(bf16[32,3072]{1,0:T(8,128)(2,1)} %param.12) | data formatting | bytes 393216 | tf_op jit(solution)/shard_map/reshape | solution.py:483
  1.5 0.2 copy-done
  1.7 0.0 copy-start.1
  1.7 0.0 copy-start.2
  1.7 0.0 copy-start.3
  1.7 0.0 copy-start.4
  1.7 0.4 fusion.1
  2.1 0.3 copy.20
  2.4 0.1 pad_maximum_fusion.q_full
  2.5 0.0 copy-done.1
  2.5 0.0 copy-done.2
  2.5 0.0 copy-done.3
  2.5 0.0 copy-done.4
  2.5 111.5 %layer.1 = bf16[32,896]{1,0:T(8,128)(2,1)S(1)} custom-call(s32[32]{0:T(128)S(1)} %copy-done.4, bf16[32,16,576]{2,1,0:T(8,128)(2,1)S(1)} %pad_maximum_fusion.q_full, bf16[32,576]{1,0:T(8,128)(2,1)S(1)} %copy-done.2, bf16[32,576,256]{2,1,0:T(8,128)(2,1)} %bitcast.7, bf16[16,512,128]{2,1,0:T(8,128)(2,1)} %value_up.1, bf16[512,896]{1,0:T(8,128)(2,1)} %out_proj.1, ...), custom_call_target="tpu_custom_call" | custom-call | tf_op jit(solution)/shard_map/layer/pallas_call | solution.py:425
  114.0 0.6 copy.22
  (2 shorter events, 0.0 us)
Async XLA Ops:
  0.0 1.7 %copy-start = (bf16[16,128,512]{2,1,0:T(8,128)(2,1)S(1)}, bf16[16,128,512]{2,1,0:T(8,128)(2,1)}, u32[]{:S(2)}) copy-start(bf16[16,128,512]{2,1,0:T(8,128)(2,1)} %param.16) | copy-start | bytes 6291460
  1.7 0.8 copy-start.1
  1.7 0.8 copy-start.2
  1.7 0.8 copy-start.3
  1.7 0.8 copy-start.4

commit v4 on v3

--- a/solution.py
+++ b/solution.py
@@ -16,7 +16,7 @@
 
 
 def layer_kernel(
-    lengths, q_full, fresh, cache, value_up, out_proj, residual, gain, gate, up, down,
+    lengths, q_latent, q_heads, fresh, cache, value_up, out_proj, residual, gain, gate, up, down,
     out,
     keys, vup, fresh_f, lat, attn, wo, wg, wu, wd, zbuf, ain, proj, rs1, sg, xn, st, stin, rcol, own, p4, z6, hid, dnb, rs2,
     c_s, v_s, w_l, w_s, w_r, z_s, z_r, a_s, a_r, p_s, p_r, g_s, g_r, t_s, t_r, z6_s, z6_r, h_s, h_r, d_s, d_r,
@@ -47,21 +47,6 @@
 
     def arrived(ref, sem):
         pltpu.make_async_copy(ref, ref, sem).wait()
-
-    barrier = pltpu.get_barrier_semaphore()
-    pl.semaphore_signal(barrier, inc=1, device_id=partner, device_id_type=MESH)
-
-    def greet_plane(d, _):
-        pl.semaphore_signal(barrier, inc=1, device_id=chip((p + d) % 16), device_id_type=MESH)
-        return 0
-
-    lax.fori_loop(1, 16, greet_plane, 0)
-
-    def greet_level(d, _):
-        pl.semaphore_signal(barrier, inc=1, device_id=level(d), device_id_type=MESH)
-        return 0
-
-    lax.fori_loop(1, 8, greet_level, 0)
 
     for g in range(GROUPS):
         rows = pl.ds(g * GROUP, GROUP)
@@ -72,6 +57,22 @@
     theirs = (wo.at[1 - c], wg.at[1 - c], wu.at[1 - c], wd.at[1 - c])
     for n, (src, dst) in enumerate(pairs):
         pltpu.make_async_copy(src, dst, w_l.at[n]).start()
+
+    barrier = pltpu.get_barrier_semaphore()
+    pl.semaphore_signal(barrier, inc=1, device_id=partner, device_id_type=MESH)
+
+    def greet_plane(d, _):
+        pl.semaphore_signal(barrier, inc=1, device_id=chip((p + d) % 16), device_id_type=MESH)
+        return 0
+
+    lax.fori_loop(1, 16, greet_plane, 0)
+
+    def greet_level(d, _):
+        pl.semaphore_signal(barrier, inc=1, device_id=level(d), device_id_type=MESH)
+        return 0
+
+    lax.fori_loop(1, 8, greet_level, 0)
+
     fresh_f[...] = fresh[...].astype(F32)
 
     def weight(n):
@@ -85,10 +86,17 @@
         scores, new_score, used = [], [], []
         for i in range(GROUP):
             r = g * GROUP + i
-            q = q_full[r]
+            q = q_latent[r]
+            turned = q_heads[r, :, 128:192]
             entry = fresh_f[pl.ds(r, 1), :]
-            scores.append(jnp.dot(q, keys[r], preferred_element_type=F32) * SCALE)
-            new_score.append(jnp.sum(q.astype(F32) * entry, axis=1, keepdims=True) * SCALE)
+            score = jnp.dot(q, keys[r, 0:512, :], preferred_element_type=F32) + jnp.dot(
+                turned, keys[r, 512:576, :], preferred_element_type=F32
+            )
+            scores.append(score * SCALE)
+            fresh_score = jnp.sum(q.astype(F32) * entry[:, 0:512], axis=1, keepdims=True) + jnp.sum(
+                turned.astype(F32) * entry[:, 512:576], axis=1, keepdims=True
+            )
+            new_score.append(fresh_score * SCALE)
             used.append(slot < lengths[r])
         masked = jnp.concatenate([jnp.where(u, v, -1e30) for u, v in zip(used, scores)], axis=0)
         new_score = jnp.concatenate(new_score, axis=0)
@@ -417,7 +425,7 @@
     settle(((dnb, d_s),), (1,))
 
 
-def layer(lengths, q_full, fresh, cache, value_up, out_proj, residual, gain, gate, up, down):
+def layer(lengths, q_latent, q_heads, fresh, cache, value_up, out_proj, residual, gain, gate, up, down):
     vm = pl.BlockSpec(memory_space=pltpu.VMEM)
     hbm = pl.BlockSpec(memory_space=pl.ANY)
     dma = pltpu.SemaphoreType.DMA
@@ -425,7 +433,7 @@
     return pl.pallas_call(
         layer_kernel,
         out_shape=jax.ShapeDtypeStruct((32, 896), BF),
-        in_specs=[pl.BlockSpec(memory_space=pltpu.SMEM), vm, vm, hbm, hbm, hbm, vm, vm, hbm, hbm, hbm],
+        in_specs=[pl.BlockSpec(memory_space=pltpu.SMEM), vm, vm, vm, hbm, hbm, hbm, vm, vm, hbm, hbm, hbm],
         out_specs=vm,
         scratch_shapes=[
             pltpu.VMEM((32, 576, 256), BF),
@@ -463,7 +471,7 @@
             collective_id=0, has_side_effects=True, vmem_limit_bytes=53 * 2**20
         ),
         name="layer",
-    )(lengths, q_full, fresh, cache, value_up, out_proj, residual, gain, gate, up, down)
+    )(lengths, q_latent, q_heads, fresh, cache, value_up, out_proj, residual, gain, gate, up, down)
 
 
 def body(
@@ -484,10 +492,10 @@
     q_latent = jnp.einsum(
         "rhk,hkl->rhl", query_heads[:, :, :128], key_up_matrix, preferred_element_type=F32
     ).astype(BF)
-    q_full = jnp.concatenate([q_latent, query_heads[:, :, 128:]], axis=2)
     return layer(
         lengths,
-        q_full,
+        q_latent,
+        query_heads,
         fresh_latent_entry,
         latent_cache.transpose(0, 2, 1),
         value_up_matrix,

time: 115 us -> 115 us (level)
  no operation moved by 1% of the time
where the time goes in v4:
time: 115 us
  Pallas kernels  111 us (97%)
  local copies, waits for them, and re-layouts  2.57 us (2%)
    pallas_call x1, Pallas kernels, layer(): pl.pallas_call(layer_kernel, out_shape=jax.ShapeDtypeStruct((32, 896), BF...  111 us

profile of v4, /device:TPU:8, one launch (start us, length us, event | category | flops | bytes accessed | tf_op | source)
XLA Modules:
  0.0 114.5 jit_solution(17150079295679637106)
XLA Ops:
  0.0 0.0 copy-start
  0.0 1.4 %reshape.3.q_heads = bf16[32,16,192]{2,1,0:T(8,128)(2,1)S(1)} reshape(bf16[32,3072]{1,0:T(8,128)(2,1)} %param.12) | data formatting | bytes 393216 | tf_op jit(solution)/shard_map/reshape | solution.py:491
  1.4 0.0 copy-start.1
  1.4 0.0 copy-start.2
  1.4 0.0 copy-start.3
  1.4 0.0 copy-start.4
  1.5 0.2 copy-done
  1.7 0.4 fusion.1
  2.1 0.3 copy.20
  2.4 0.0 copy-done.1
  2.4 0.0 copy-done.2
  2.4 0.0 copy-done.3
  2.4 0.0 copy-done.4
  2.4 111.5 %layer.1 = bf16[32,896]{1,0:T(8,128)(2,1)S(1)} custom-call(s32[32]{0:T(128)S(1)} %copy-done.4, bf16[32,16,512]{2,1,0:T(8,128)(2,1)S(1)} %bitcast.7, bf16[32,16,192]{2,1,0:T(8,128)(2,1)S(1)} %reshape.3.q_heads, bf16[32,576]{1,0:T(8,128)(2,1)S(1)} %copy-done.2, bf16[32,576,256]{2,1,0:T(8,128)(2,1)} %bitcast.8, bf16[16,512,128]{2,1,0:T(8,128)(2,1)} %value_up.1, ...), custom_call_target="tpu_custom_call" | custom-call | tf_op jit(solution)/shard_map/layer/pallas_call | solution.py:433
  113.9 0.6 copy.22
  (1 shorter events, 0.0 us)
Async XLA Ops:
  0.0 1.7 %copy-start = (bf16[16,128,512]{2,1,0:T(8,128)(2,1)S(1)}, bf16[16,128,512]{2,1,0:T(8,128)(2,1)}, u32[]{:S(2)}) copy-start(bf16[16,128,512]{2,1,0:T(8,128)(2,1)} %param.16) | copy-start | bytes 6291460
  1.4 1.0 copy-start.1
  1.4 1.0 copy-start.2
  1.4 1.0 copy-start.3
  1.4 1.0 copy-start.4
